TPU v7x, 256 devices: a whole 4x4x8 slice. The times are simulated.
256 devices in a mesh: quad: 8 (over z_lo, core), dom: 32 (over x, y, z_hi).
Axes of the slice: x: 4, y: 4, z: 8 (z_hi: 2, z_lo: 4; z = z_hi * 4 + z_lo), core: 2. Of those that a mesh axis runs over, the one named last changes fastest.
Arguments:
- probes: float32 [2, 64, 256, 128], P(None, None, 'dom'), may hold values from -6 to 6
- mass_weights: float32 [256, 128], P('dom'), may hold values from 0.8 to 1.25
- blocks: float32 [2, 256, 128, 128], P(None, 'dom'), may hold values from -4 to 4
- couplings: float32 [2, 6, 256, 128], P(None, None, 'dom'), may hold values from -0.25 to 0.25
Outputs:
- moments: float32 [64, 4, 2, 256, 128], P('quad', None, None, 'dom')
- projected: float32 [2, 8, 64, 64], replicated
All inputs are finite; a program needn't handle non-finite values.
Results may differ from a plain program's by a relative error of at most 0.0001.
Values sent between devices are 32-bit elements; how exact they have to be, the bound alone decides.
A program may use at most 64 MiB of HBM per device.

v0:
```python
import math
import jax
import jax.numpy as jnp
from jax import lax
from jax.sharding import PartitionSpec as P

NQ = 16
ITERS = 4
MOM = 4
PRECISE = lax.Precision.HIGHEST
RADIUS = 2.0
OFFSETS = (-3, -2, -1, 1, 2, 3)


def with_halo(cells, sides, width):
    for axis, dim in sides:
        count = lax.axis_size(axis)
        ends = count - 1
        head = lax.slice_in_dim(cells, 0, width, axis=dim)
        tail = lax.slice_in_dim(cells, cells.shape[dim] - width, cells.shape[dim], axis=dim)
        cells = jnp.concatenate(
            [
                lax.ppermute(tail, axis, [(i, (i + 1) % count) for i in range(ends)]),
                cells,
                lax.ppermute(head, axis, [((i + 1) % count, i) for i in range(ends)]),
            ],
            axis=dim,
        )
    return cells


def shift_angles(shift_index, total_shifts):
    return 2.0 * math.pi / total_shifts * (shift_index.astype(jnp.float32) + 0.5)


def moment_weights(angles, moment_count, scale):
    orders = jnp.arange(1, moment_count + 1, dtype=jnp.float32)
    phases = orders[:, None] * angles[None, :]
    return (scale * jnp.cos(phases), scale * jnp.sin(phases))


def sweep(field, padded, blocks, couplings, zmass_re, zmass_im, inverse_re, inverse_im, source):
    rim_depth = max(OFFSETS)
    line_count = field.shape[3]
    field_re = field[0]
    field_im = field[1]
    image_re = jnp.einsum("spxj,xij->spxi", field_re, blocks[0], precision=PRECISE) - jnp.einsum(
        "spxj,xij->spxi", field_im, blocks[1], precision=PRECISE
    )
    image_im = jnp.einsum("spxj,xij->spxi", field_im, blocks[0], precision=PRECISE) + jnp.einsum(
        "spxj,xij->spxi", field_re, blocks[1], precision=PRECISE
    )
    for position, offset in enumerate(OFFSETS):
        neighbour = padded[:, :, :, rim_depth + offset : rim_depth + offset + line_count]
        coup_re = couplings[0, position]
        coup_im = couplings[1, position]
        image_re = image_re + coup_re * neighbour[0] - coup_im * neighbour[1]
        image_im = image_im + coup_re * neighbour[1] + coup_im * neighbour[0]
    resid_re = source[0] - (zmass_re * field_re - zmass_im * field_im) + image_re
    resid_im = source[1] - (zmass_re * field_im + zmass_im * field_re) + image_im
    return jnp.stack(
        [
            field_re + resid_re * inverse_re - resid_im * inverse_im,
            field_im + resid_re * inverse_im + resid_im * inverse_re,
        ]
    )


def moment_block(field_part, weight_re, weight_im):
    sum_re = jnp.einsum("ks,spxi->pkxi", weight_re, field_part[0], precision=PRECISE) - jnp.einsum(
        "ks,spxi->pkxi", weight_im, field_part[1], precision=PRECISE
    )
    sum_im = jnp.einsum("ks,spxi->pkxi", weight_re, field_part[1], precision=PRECISE) + jnp.einsum(
        "ks,spxi->pkxi", weight_im, field_part[0], precision=PRECISE
    )
    return jnp.stack([sum_re, sum_im], axis=2)


def project(gram_re, gram_im, angles, scale):
    proj_re, proj_im = moment_weights(angles, 2 * MOM, scale)
    mixed_re = jnp.einsum("ks,spq->kpq", proj_re, gram_re, precision=PRECISE) - jnp.einsum(
        "ks,spq->kpq", proj_im, gram_im, precision=PRECISE
    )
    mixed_im = jnp.einsum("ks,spq->kpq", proj_re, gram_im, precision=PRECISE) + jnp.einsum(
        "ks,spq->kpq", proj_im, gram_re, precision=PRECISE
    )
    return jnp.stack([mixed_re, mixed_im])


def on_device(probes, mass_weights, blocks, couplings):
    rim_depth = max(OFFSETS)
    shift_count = NQ // lax.axis_size("quad")
    probe_count = probes.shape[1]
    owned_probes = probe_count // lax.axis_size("quad")
    line_count = probes.shape[2]
    row_width = probes.shape[3]
    total_lines = line_count * lax.axis_size("dom")
    shift_index = lax.axis_index("quad") * shift_count + jnp.arange(shift_count, dtype=jnp.int32)
    angles = shift_angles(shift_index, NQ)
    zmass_re = (RADIUS * jnp.cos(angles))[:, None, None, None] * mass_weights[None, None]
    zmass_im = (RADIUS * jnp.sin(angles))[:, None, None, None] * mass_weights[None, None]
    diagonal = jnp.diagonal(blocks, axis1=2, axis2=3)
    denom_re = zmass_re - diagonal[0]
    denom_im = zmass_im - diagonal[1]
    modulus = denom_re * denom_re + denom_im * denom_im
    inverse_re = denom_re / modulus
    inverse_im = -denom_im / modulus
    source = mass_weights[None, None] * probes
    field = jnp.stack(
        [
            source[0] * inverse_re - source[1] * inverse_im,
            source[0] * inverse_im + source[1] * inverse_re,
        ]
    )
    for step in range(ITERS - 1):
        padded = with_halo(field, (("dom", 3),), rim_depth)
        field = sweep(
            field, padded, blocks, couplings, zmass_re, zmass_im, inverse_re, inverse_im, source
        )
    weight_re, weight_im = moment_weights(angles, MOM, RADIUS / NQ)
    field_rows = lax.slice_in_dim(field, 0, owned_probes * lax.axis_size("quad"), axis=2)
    moments = lax.psum_scatter(
        moment_block(field_rows, weight_re, weight_im), "quad", scatter_dimension=0, tiled=True
    )
    gram_re = jnp.einsum("pxi,sqxi->spq", probes[0], field[0], precision=PRECISE) + jnp.einsum(
        "pxi,sqxi->spq", probes[1], field[1], precision=PRECISE
    )
    gram_im = jnp.einsum("pxi,sqxi->spq", probes[0], field[1], precision=PRECISE) - jnp.einsum(
        "pxi,sqxi->spq", probes[1], field[0], precision=PRECISE
    )
    scale = RADIUS / (NQ * total_lines * row_width)
    projected = lax.psum(project(gram_re, gram_im, angles, scale), ("quad", "dom"))
    return (moments, projected)


def solution(mesh):
    return jax.shard_map(
        on_device,
        mesh=mesh,
        in_specs=(
            P(None, None, "dom", None),
            P("dom", None),
            P(None, "dom", None, None),
            P(None, None, "dom", None),
        ),
        out_specs=(P("quad", None, None, "dom", None), P()),
        check_vma=False,
    )
```

profile of v0, /device:TPU:2, one launch (start us, length us, event | category | flops | bytes accessed | tf_op | source)
XLA Modules:
  0.0 444.9 jit_solution(10704677841827037540)
XLA Ops:
  8.0 0.0 all-reduce.2.cloned.1.call-start
  8.1 0.0 copy-start.3
  8.1 13.3 %copy.50 = f32[2,8,128,128]{1,0,3,2:T(2,128)} copy(f32[2,8,128,128]{3,2,1,0:T(8,128)} %param.6) | data formatting | bytes 2097152 | tf_op args[2]
  21.3 6.7 %gather_fusion = f32[128,2,8]{2,1,0:T(2,128)S(1)} fusion(f32[2,8,128,128]{1,0,3,2:T(2,128)} %copy.50, s32[128]{0:T(128)S(1)} %or_bitcast_fusion), kind=kCustom, calls=%fused_computation | custom fusion | bytes 17408 | tf_op jit(solution)/shard_map/jit(diagonal)/gather | solution.py:102
  28.0 0.1 fusion.130
  28.2 0.1 copy.51
  28.3 0.1 sine_multiply_fusion
  28.4 0.1 copy.53
  28.5 0.1 copy.49
  28.6 0.1 fusion.78
  28.7 0.0 copy-start
  28.7 0.2 multiply_subtract_fusion.3
  28.8 0.1 pad_maximum_fusion.9
  28.9 11.7 %collective-permute-start.1 = (f32[2,2,64,3,128]{4,2,1,3,0:T(8,128)S(1)}, f32[2,2,64,3,128]{4,2,1,3,0:T(8,128)S(1)}, u32[]{:S(2)}, u32[]{:S(2)}) collective-permute-start(f32[2,2,64,3,128]{4,2,1,3,0:T(8,128)S(1)} %get-tuple-element.24), channel_id=1, source_target_pairs={{1,0},{2,1},{3,2},{4,3},{5,4},{6,5},{7,6},{8,7},{9,8},{10,9},{11,1... | collective-permute-start | bytes 1179656 | tf_op jit(solution)/shard_map/ppermute | solution.py:25
  40.6 1.9 collective-permute-start
  42.5 1.2 fusion.30
  43.9 1.2 fusion.28
  45.1 7.2 %collective-permute-done.1 = f32[2,2,64,3,128]{4,2,1,3,0:T(8,128)S(1)} collective-permute-done((f32[2,2,64,3,128]{4,2,1,3,0:T(8,128)S(1)}, f32[2,2,64,3,128]{4,2,1,3,0:T(8,128)S(1)}, u32[]{:S(2)}, u32[]{:S(2)}) %collective-permute-start.1) | collective-permute-done | bytes 393248 | tf_op jit(solution)/shard_map/ppermute | solution.py:25
  52.3 21.3 %collective-permute-done = f32[2,2,64,3,128]{4,2,1,3,0:T(8,128)S(1)} collective-permute-done((f32[2,2,64,3,128]{4,2,1,3,0:T(8,128)S(1)}, f32[2,2,64,3,128]{4,2,1,3,0:T(8,128)S(1)}, u32[]{:S(2)}, u32[]{:S(2)}) %collective-permute-start) | collective-permute-done | bytes 393248 | tf_op jit(solution)/shard_map/ppermute | solution.py:23
  73.6 0.4 pad_maximum_fusion.1
  74.0 1.9 subtract_add_fusion.2
  75.9 2.2 multiply_add_fusion.2
  78.1 0.1 pad_maximum_fusion.7
  78.2 8.9 %collective-permute-start.3 = (f32[2,2,64,3,128]{4,2,1,3,0:T(8,128)S(1)}, f32[2,2,64,3,128]{4,2,1,3,0:T(8,128)S(1)}, u32[]{:S(2)}, u32[]{:S(2)}) collective-permute-start(f32[2,2,64,3,128]{4,2,1,3,0:T(8,128)S(1)} %get-tuple-element.20), channel_id=1, source_target_pairs={{1,0},{2,1},{3,2},{4,3},{5,4},{6,5},{7,6},{8,7},{9,8},{10,9},{11,1... | collective-permute-start | bytes 1179656 | tf_op jit(solution)/shard_map/ppermute | solution.py:25
  87.1 1.9 collective-permute-start.2
  89.0 1.2 fusion.26
  90.3 1.2 fusion.24
  91.5 12.3 %collective-permute-done.3 = f32[2,2,64,3,128]{4,2,1,3,0:T(8,128)S(1)} collective-permute-done((f32[2,2,64,3,128]{4,2,1,3,0:T(8,128)S(1)}, f32[2,2,64,3,128]{4,2,1,3,0:T(8,128)S(1)}, u32[]{:S(2)}, u32[]{:S(2)}) %collective-permute-start.3) | collective-permute-done | bytes 393248 | tf_op jit(solution)/shard_map/ppermute | solution.py:25
  103.8 8.8 %collective-permute-done.2 = f32[2,2,64,3,128]{4,2,1,3,0:T(8,128)S(1)} collective-permute-done((f32[2,2,64,3,128]{4,2,1,3,0:T(8,128)S(1)}, f32[2,2,64,3,128]{4,2,1,3,0:T(8,128)S(1)}, u32[]{:S(2)}, u32[]{:S(2)}) %collective-permute-start.2) | collective-permute-done | bytes 393248 | tf_op jit(solution)/shard_map/ppermute | solution.py:23
  112.6 0.4 pad_maximum_fusion.2
  112.9 1.8 subtract_add_fusion.1
  114.8 2.1 multiply_add_fusion.1
  116.8 0.1 pad_maximum_fusion.5
  116.9 7.4 %collective-permute-start.5 = (f32[2,2,64,3,128]{4,2,1,3,0:T(8,128)S(1)}, f32[2,2,64,3,128]{4,2,1,3,0:T(8,128)S(1)}, u32[]{:S(2)}, u32[]{:S(2)}) collective-permute-start(f32[2,2,64,3,128]{4,2,1,3,0:T(8,128)S(1)} %get-tuple-element.16), channel_id=1, source_target_pairs={{1,0},{2,1},{3,2},{4,3},{5,4},{6,5},{7,6},{8,7},{9,8},{10,9},{11,1... | collective-permute-start | bytes 1179656 | tf_op jit(solution)/shard_map/ppermute | solution.py:25
  124.3 3.7 collective-permute-start.4
  128.1 1.2 fusion.22
  129.3 1.2 fusion.20
  130.5 1.3 collective-permute-done.5
  131.8 22.8 %collective-permute-done.4 = f32[2,2,64,3,128]{4,2,1,3,0:T(8,128)S(1)} collective-permute-done((f32[2,2,64,3,128]{4,2,1,3,0:T(8,128)S(1)}, f32[2,2,64,3,128]{4,2,1,3,0:T(8,128)S(1)}, u32[]{:S(2)}, u32[]{:S(2)}) %collective-permute-start.4) | collective-permute-done | bytes 393248 | tf_op jit(solution)/shard_map/ppermute | solution.py:23
  154.6 0.3 pad_maximum_fusion.3
  154.8 1.9 subtract_add_fusion
  156.8 2.1 multiply_subtract_fusion
  158.8 2.2 fusion.36
  161.0 2.2 fusion.40
  163.2 0.6 convolution_bitcast_fusion
  163.8 0.6 convolution_bitcast_fusion.2
  164.4 2.5 fusion
  166.9 2.3 fusion.1
  169.2 0.6 fusion.13
  169.8 0.1 copy.64
  169.9 0.6 fusion.11
  170.5 0.1 copy.63
  170.6 0.5 fusion.89
  171.1 0.5 fusion.91
  171.7 0.5 fusion.9
  172.2 0.5 fusion.8
  172.7 0.8 pad_maximum_fusion.4
  173.6 0.0 all-reduce.2.cloned.1.call-update
  173.6 0.0 reduce-scatter.2.cloned.1.call-start
  173.7 0.5 pad_maximum_fusion
  174.2 1.5 copy.60
  175.7 0.0 reduce-scatter.2.cloned.1.call-update
  175.8 259.7 %all-reduce.2.cloned.1.call-done = f32[2,8,64,64]{3,1,2,0:T(8,128)} async-done(((f32[2,8,64,64]{3,1,2,0:T(8,128)}), f32[2,8,64,64]{3,1,2,0:T(8,128)}) %all-reduce.2.cloned.1.call-update) | async-done | bytes 262160 | tf_op jit(solution)/shard_map/psum | solution.py:132
  435.5 1.9 copy.67
  (16 shorter events, 0.2 us)
Async XLA Ops:
  8.0 427.5 %all-reduce.2.cloned.1.call-start = ((), (), s32[]{:S(2)}) async-start(), calls=%async_computation.2 | async-start | bytes 1048576 | tf_op jit(solution)/shard_map/psum | solution.py:132
  8.1 20.3 %copy-start.1 = (f32[2,64,8,128]{3,2,1,0:T(8,128)S(1)}, f32[2,64,8,128]{3,2,1,0:T(8,128)}, u32[]{:S(2)}) copy-start(f32[2,64,8,128]{3,2,1,0:T(8,128)} %param.4) | copy-start | bytes 1572868
  8.1 20.3 %copy-start.3 = (f32[8,128]{1,0:T(8,128)S(1)}, f32[8,128]{1,0:T(8,128)}, u32[]{:S(2)}) copy-start(f32[8,128]{1,0:T(8,128)} %param.5) | copy-start | bytes 12292
  28.7 13.9 %copy-start = (f32[2,8,128,128]{3,2,1,0:T(8,128)S(1)}, f32[2,8,128,128]{3,2,1,0:T(8,128)}, u32[]{:S(2)}) copy-start(f32[2,8,128,128]{3,2,1,0:T(8,128)} %param.6) | copy-start | bytes 3145732
  28.9 14.9 %copy-start.2 = (f32[2,6,8,128]{3,2,1,0:T(8,128)S(1)}, f32[2,6,8,128]{3,2,1,0:T(8,128)}, u32[]{:S(2)}) copy-start(f32[2,6,8,128]{3,2,1,0:T(8,128)} %param.7) | copy-start | bytes 147460
  28.9 23.3 %collective-permute-start.1 = (f32[2,2,64,3,128]{4,2,1,3,0:T(8,128)S(1)}, f32[2,2,64,3,128]{4,2,1,3,0:T(8,128)S(1)}, u32[]{:S(2)}, u32[]{:S(2)}) collective-permute-start(f32[2,2,64,3,128]{4,2,1,3,0:T(8,128)S(1)} %get-tuple-element.24), channel_id=1, source_target_pairs={{1,0},{2,1},{3,2},{4,3},{5,4},{6,5},{7,6},{8,7},{9,8},{10,9},{11,1... | collective-permute-start | bytes 1179656 | tf_op jit(solution)/shard_map/ppermute | solution.py:25
  40.6 33.0 %collective-permute-start = (f32[2,2,64,3,128]{4,2,1,3,0:T(8,128)S(1)}, f32[2,2,64,3,128]{4,2,1,3,0:T(8,128)S(1)}, u32[]{:S(2)}, u32[]{:S(2)}) collective-permute-start(f32[2,2,64,3,128]{4,2,1,3,0:T(8,128)S(1)} %get-tuple-element.25), channel_id=1, source_target_pairs={{0,1},{1,2},{2,3},{3,4},{4,5},{5,6},{6,7},{7,8},{8,9},{9,10},{10,1... | collective-permute-start | bytes 1179656 | tf_op jit(solution)/shard_map/ppermute | solution.py:23
  78.2 25.6 %collective-permute-start.3 = (f32[2,2,64,3,128]{4,2,1,3,0:T(8,128)S(1)}, f32[2,2,64,3,128]{4,2,1,3,0:T(8,128)S(1)}, u32[]{:S(2)}, u32[]{:S(2)}) collective-permute-start(f32[2,2,64,3,128]{4,2,1,3,0:T(8,128)S(1)} %get-tuple-element.20), channel_id=1, source_target_pairs={{1,0},{2,1},{3,2},{4,3},{5,4},{6,5},{7,6},{8,7},{9,8},{10,9},{11,1... | collective-permute-start | bytes 1179656 | tf_op jit(solution)/shard_map/ppermute | solution.py:25
  87.1 25.5 %collective-permute-start.2 = (f32[2,2,64,3,128]{4,2,1,3,0:T(8,128)S(1)}, f32[2,2,64,3,128]{4,2,1,3,0:T(8,128)S(1)}, u32[]{:S(2)}, u32[]{:S(2)}) collective-permute-start(f32[2,2,64,3,128]{4,2,1,3,0:T(8,128)S(1)} %get-tuple-element.21), channel_id=1, source_target_pairs={{0,1},{1,2},{2,3},{3,4},{4,5},{5,6},{6,7},{7,8},{8,9},{9,10},{10,1... | collective-permute-start | bytes 1179656 | tf_op jit(solution)/shard_map/ppermute | solution.py:23
  116.9 14.9 %collective-permute-start.5 = (f32[2,2,64,3,128]{4,2,1,3,0:T(8,128)S(1)}, f32[2,2,64,3,128]{4,2,1,3,0:T(8,128)S(1)}, u32[]{:S(2)}, u32[]{:S(2)}) collective-permute-start(f32[2,2,64,3,128]{4,2,1,3,0:T(8,128)S(1)} %get-tuple-element.16), channel_id=1, source_target_pairs={{1,0},{2,1},{3,2},{4,3},{5,4},{6,5},{7,6},{8,7},{9,8},{10,9},{11,1... | collective-permute-start | bytes 1179656 | tf_op jit(solution)/shard_map/ppermute | solution.py:25
  124.3 30.2 %collective-permute-start.4 = (f32[2,2,64,3,128]{4,2,1,3,0:T(8,128)S(1)}, f32[2,2,64,3,128]{4,2,1,3,0:T(8,128)S(1)}, u32[]{:S(2)}, u32[]{:S(2)}) collective-permute-start(f32[2,2,64,3,128]{4,2,1,3,0:T(8,128)S(1)} %get-tuple-element.17), channel_id=1, source_target_pairs={{0,1},{1,2},{2,3},{3,4},{4,5},{5,6},{6,7},{7,8},{8,9},{9,10},{10,1... | collective-permute-start | bytes 1179656 | tf_op jit(solution)/shard_map/ppermute | solution.py:23
  173.6 263.8 %reduce-scatter.2.cloned.1.call-start = ((), (), s32[]{:S(2)}) async-start(), calls=%async_computation.1 | async-start | bytes 2359296 | tf_op jit(solution)/shard_map/reduce_scatter | solution.py:122
Sparse Core Ops, SparseCore 0:
  173.7 261.7 all-reduce.1
Sparse Core Ops, SparseCore 1:
  177.2 49.0 reduce-scatter.1
where the time goes:
time: 446 us; the launch traced here: 445 us
  waiting for transfers between devices  333 us (75%)
  starting transfers between devices  35.6 us (8%)
  matrix products  32.9 us (7%)
  local copies, waits for them, and re-layouts  24 us (5%)
  between operations  15.9 us (4%)
    psum x1, waiting for transfers between devices, on_device(): lax.psum(project(gram_re, gram_im, angles, scale), ('quad', 'dom'))  260 us
    ppermute x3, waiting for transfers between devices, with_halo(): lax.ppermute(tail, axis, [(i, (i + 1) % count) for i in range(ends)])  52.9 us
    ppermute x3, starting transfers between devices, with_halo(): lax.ppermute(head, axis, [((i + 1) % count, i) for i in range(ends)])  28 us
    ppermute x3, waiting for transfers between devices, with_halo(): lax.ppermute(head, axis, [((i + 1) % count, i) for i in range(ends)])  20.8 us
    unnamed x10, local copies, waits for them, and re-layouts  15.2 us
  transfers between devices with their start and end apart: 8, of which 7 were waited for; matrix products, arithmetic and copies ran while one was open for 3% of the time, Pallas kernels for 0%

commit v1 on v0

--- a/solution.py
+++ b/solution.py
@@ -129,7 +129,8 @@
         "pxi,sqxi->spq", probes[1], field[0], precision=PRECISE
     )
     scale = RADIUS / (NQ * total_lines * row_width)
-    projected = lax.psum(project(gram_re, gram_im, angles, scale), ("quad", "dom"))
+    inner = lax.psum(project(gram_re, gram_im, angles, scale), "dom")
+    projected = lax.psum(inner, "quad")
     return (moments, projected)
 
 

time: 446 us -> 727 us (1.63)
  waiting for transfers between devices: 333 us -> 617 us
    psum x1 -> x2, waiting for transfers between devices: 260 us -> 502 us  [the longest x1 427 us: on_device(): inner = lax.psum(project(gram_re, gram_im, angles, scale), 'dom')]
    reduce_scatter x1, waiting for transfers between devices: 0.01 us -> 41.3 us  [on_device(): lax.psum_scatter(moment_block(field_rows, weight_re, weight_im), 'quad',...]
  transfers between devices with their start and end apart: 8 -> 9, of which waited for: 7 -> 9; matrix products, arithmetic and copies ran while one was open for 3% -> 2% of each run, Pallas kernels for 0% -> 0%
where the time goes in v1:
time: 727 us; the launch traced here: 726 us
  waiting for transfers between devices  617 us (85%)
  starting transfers between devices  35.8 us (5%)
  matrix products  32.7 us (4%)
  local copies, waits for them, and re-layouts  24 us (3%)
  between operations  14.2 us (2%)
    psum x1, waiting for transfers between devices, on_device(): inner = lax.psum(project(gram_re, gram_im, angles, scale), 'dom')  427 us
    psum x1, waiting for transfers between devices, on_device(): projected = lax.psum(inner, 'quad')  74.4 us
    ppermute x3, waiting for transfers between devices, with_halo(): lax.ppermute(tail, axis, [(i, (i + 1) % count) for i in range(ends)])  52.1 us
    reduce_scatter x1, waiting for transfers between devices, on_device(): lax.psum_scatter(moment_block(field_rows, weight_re, weight_im), 'quad',...  41.3 us
    ppermute x3, starting transfers between devices, with_halo(): lax.ppermute(head, axis, [((i + 1) % count, i) for i in range(ends)])  28 us
    ppermute x3, waiting for transfers between devices, with_halo(): lax.ppermute(head, axis, [((i + 1) % count, i) for i in range(ends)])  21.4 us
    unnamed x10, local copies, waits for them, and re-layouts  15.2 us
  transfers between devices with their start and end apart: 9, of which 9 were waited for; matrix products, arithmetic and copies ran while one was open for 2% of the time, Pallas kernels for 0%

profile of v1, /device:TPU:2, one launch (start us, length us, event | category | flops | bytes accessed | tf_op | source)
XLA Modules:
  0.0 726.2 jit_solution(16526051203622561968)
XLA Ops:
  7.2 0.0 all-reduce.3.cloned.1.call-start
  7.2 13.3 %copy.50 = f32[2,8,128,128]{1,0,3,2:T(2,128)} copy(f32[2,8,128,128]{3,2,1,0:T(8,128)} %param.6) | data formatting | bytes 2097152 | tf_op args[2]
  20.5 6.7 gather_fusion
  27.2 0.1 fusion.130
  27.4 0.1 copy.51
  27.4 0.1 sine_multiply_fusion
  27.6 0.1 copy.53
  27.7 0.1 copy.49
  27.7 0.1 fusion.78
  27.8 0.1 multiply_subtract_fusion.3
  28.0 0.1 pad_maximum_fusion.9
  28.1 11.7 %collective-permute-start.1 = (f32[2,2,64,3,128]{4,2,1,3,0:T(8,128)S(1)}, f32[2,2,64,3,128]{4,2,1,3,0:T(8,128)S(1)}, u32[]{:S(2)}, u32[]{:S(2)}) collective-permute-start(f32[2,2,64,3,128]{4,2,1,3,0:T(8,128)S(1)} %get-tuple-element.24), channel_id=1, source_target_pairs={{1,0},{2,1},{3,2},{4,3},{5,4},{6,5},{7,6},{8,7},{9,8},{10,9},{11,1... | collective-permute-start | bytes 1179656 | tf_op jit(solution)/shard_map/ppermute | solution.py:25
  39.7 1.9 collective-permute-start
  41.7 1.2 fusion.30
  43.0 1.2 fusion.28
  44.2 7.2 collective-permute-done.1
  51.4 21.3 %collective-permute-done = f32[2,2,64,3,128]{4,2,1,3,0:T(8,128)S(1)} collective-permute-done((f32[2,2,64,3,128]{4,2,1,3,0:T(8,128)S(1)}, f32[2,2,64,3,128]{4,2,1,3,0:T(8,128)S(1)}, u32[]{:S(2)}, u32[]{:S(2)}) %collective-permute-start) | collective-permute-done | bytes 393248 | tf_op jit(solution)/shard_map/ppermute | solution.py:23
  72.7 0.4 pad_maximum_fusion.1
  73.1 1.9 subtract_add_fusion.2
  75.0 2.2 multiply_add_fusion.2
  77.2 0.1 pad_maximum_fusion.7
  77.3 8.9 %collective-permute-start.3 = (f32[2,2,64,3,128]{4,2,1,3,0:T(8,128)S(1)}, f32[2,2,64,3,128]{4,2,1,3,0:T(8,128)S(1)}, u32[]{:S(2)}, u32[]{:S(2)}) collective-permute-start(f32[2,2,64,3,128]{4,2,1,3,0:T(8,128)S(1)} %get-tuple-element.20), channel_id=1, source_target_pairs={{1,0},{2,1},{3,2},{4,3},{5,4},{6,5},{7,6},{8,7},{9,8},{10,9},{11,1... | collective-permute-start | bytes 1179656 | tf_op jit(solution)/shard_map/ppermute | solution.py:25
  86.2 1.9 collective-permute-start.2
  88.2 1.2 fusion.26
  89.4 1.2 fusion.24
  90.6 12.9 %collective-permute-done.3 = f32[2,2,64,3,128]{4,2,1,3,0:T(8,128)S(1)} collective-permute-done((f32[2,2,64,3,128]{4,2,1,3,0:T(8,128)S(1)}, f32[2,2,64,3,128]{4,2,1,3,0:T(8,128)S(1)}, u32[]{:S(2)}, u32[]{:S(2)}) %collective-permute-start.3) | collective-permute-done | bytes 393248 | tf_op jit(solution)/shard_map/ppermute | solution.py:25
  103.5 8.1 %collective-permute-done.2 = f32[2,2,64,3,128]{4,2,1,3,0:T(8,128)S(1)} collective-permute-done((f32[2,2,64,3,128]{4,2,1,3,0:T(8,128)S(1)}, f32[2,2,64,3,128]{4,2,1,3,0:T(8,128)S(1)}, u32[]{:S(2)}, u32[]{:S(2)}) %collective-permute-start.2) | collective-permute-done | bytes 393248 | tf_op jit(solution)/shard_map/ppermute | solution.py:23
  111.6 0.4 pad_maximum_fusion.2
  112.0 1.8 subtract_add_fusion.1
  113.8 2.0 multiply_add_fusion.1
  115.8 0.1 pad_maximum_fusion.5
  115.9 7.5 %collective-permute-start.5 = (f32[2,2,64,3,128]{4,2,1,3,0:T(8,128)S(1)}, f32[2,2,64,3,128]{4,2,1,3,0:T(8,128)S(1)}, u32[]{:S(2)}, u32[]{:S(2)}) collective-permute-start(f32[2,2,64,3,128]{4,2,1,3,0:T(8,128)S(1)} %get-tuple-element.16), channel_id=1, source_target_pairs={{1,0},{2,1},{3,2},{4,3},{5,4},{6,5},{7,6},{8,7},{9,8},{10,9},{11,1... | collective-permute-start | bytes 1179656 | tf_op jit(solution)/shard_map/ppermute | solution.py:25
  123.3 3.8 collective-permute-start.4
  127.1 1.2 fusion.22
  128.3 1.2 fusion.20
  129.6 1.3 collective-permute-done.5
  130.9 22.7 %collective-permute-done.4 = f32[2,2,64,3,128]{4,2,1,3,0:T(8,128)S(1)} collective-permute-done((f32[2,2,64,3,128]{4,2,1,3,0:T(8,128)S(1)}, f32[2,2,64,3,128]{4,2,1,3,0:T(8,128)S(1)}, u32[]{:S(2)}, u32[]{:S(2)}) %collective-permute-start.4) | collective-permute-done | bytes 393248 | tf_op jit(solution)/shard_map/ppermute | solution.py:23
  153.6 0.4 pad_maximum_fusion.3
  153.9 1.8 subtract_add_fusion
  155.7 2.0 multiply_subtract_fusion
  157.8 0.6 convolution_bitcast_fusion
  158.3 0.6 convolution_bitcast_fusion.2
  158.9 2.2 fusion.36
  161.1 2.4 fusion
  163.5 0.6 fusion.13
  164.0 0.1 copy.64
  164.1 0.6 fusion.11
  164.7 0.1 copy.63
  164.8 0.5 fusion.89
  165.4 0.5 fusion.91
  165.9 0.8 fusion.9
  166.7 0.5 fusion.8
  167.2 0.8 pad_maximum_fusion.4
  168.1 0.0 all-reduce.5.cloned.1.call-start
  168.2 2.2 fusion.40
  170.4 427.3 %all-reduce.3.cloned.1.call-done = f32[2,8,64,64]{3,1,2,0:T(8,128)} async-done(((f32[2,8,64,64]{3,1,2,0:T(8,128)}), f32[2,8,64,64]{3,1,2,0:T(8,128)}) %all-reduce.3.cloned.1.call-update) | async-done | bytes 262160 | tf_op jit(solution)/shard_map/psum | solution.py:132
  597.7 0.0 all-reduce.5.cloned.1.call-update
  597.7 0.0 reduce-scatter.2.cloned.1.call-start
  597.8 2.2 fusion.1
  600.0 0.5 pad_maximum_fusion
  600.6 1.5 copy.60
  602.1 74.4 %all-reduce.5.cloned.1.call-done = f32[2,8,64,64]{3,1,2,0:T(8,128)} async-done(((f32[2,8,64,64]{3,1,2,0:T(8,128)}), f32[2,8,64,64]{3,1,2,0:T(8,128)}) %all-reduce.5.cloned.1.call-update) | async-done | bytes 262160 | tf_op jit(solution)/shard_map/psum | solution.py:133
  676.5 1.9 copy.67
  678.4 41.3 %reduce-scatter.2.cloned.1.call-done = f32[8,4,2,8,128]{4,3,2,1,0:T(8,128)} async-done(((f32[64,4,2,8,128]{4,3,2,1,0:T(8,128)}), f32[8,4,2,8,128]{4,3,2,1,0:T(8,128)}) %reduce-scatter.2.cloned.1.call-update) | async-done | bytes 262160 | tf_op jit(solution)/shard_map/reduce_scatter | solution.py:122
  (19 shorter events, 0.3 us)
Async XLA Ops:
  7.2 590.5 %all-reduce.3.cloned.1.call-start = ((), (), s32[]{:S(2)}) async-start(), calls=%async_computation.2 | async-start | bytes 1048576 | tf_op jit(solution)/shard_map/psum | solution.py:132
  7.2 20.3 %copy-start.1 = (f32[2,64,8,128]{3,2,1,0:T(8,128)S(1)}, f32[2,64,8,128]{3,2,1,0:T(8,128)}, u32[]{:S(2)}) copy-start(f32[2,64,8,128]{3,2,1,0:T(8,128)} %param.4) | copy-start | bytes 1572868
  7.2 20.3 %copy-start.3 = (f32[8,128]{1,0:T(8,128)S(1)}, f32[8,128]{1,0:T(8,128)}, u32[]{:S(2)}) copy-start(f32[8,128]{1,0:T(8,128)} %param.5) | copy-start | bytes 12292
  27.8 13.8 %copy-start = (f32[2,8,128,128]{3,2,1,0:T(8,128)S(1)}, f32[2,8,128,128]{3,2,1,0:T(8,128)}, u32[]{:S(2)}) copy-start(f32[2,8,128,128]{3,2,1,0:T(8,128)} %param.6) | copy-start | bytes 3145732
  28.1 14.9 %copy-start.2 = (f32[2,6,8,128]{3,2,1,0:T(8,128)S(1)}, f32[2,6,8,128]{3,2,1,0:T(8,128)}, u32[]{:S(2)}) copy-start(f32[2,6,8,128]{3,2,1,0:T(8,128)} %param.7) | copy-start | bytes 147460
  28.1 23.3 %collective-permute-start.1 = (f32[2,2,64,3,128]{4,2,1,3,0:T(8,128)S(1)}, f32[2,2,64,3,128]{4,2,1,3,0:T(8,128)S(1)}, u32[]{:S(2)}, u32[]{:S(2)}) collective-permute-start(f32[2,2,64,3,128]{4,2,1,3,0:T(8,128)S(1)} %get-tuple-element.24), channel_id=1, source_target_pairs={{1,0},{2,1},{3,2},{4,3},{5,4},{6,5},{7,6},{8,7},{9,8},{10,9},{11,1... | collective-permute-start | bytes 1179656 | tf_op jit(solution)/shard_map/ppermute | solution.py:25
  39.7 33.0 %collective-permute-start = (f32[2,2,64,3,128]{4,2,1,3,0:T(8,128)S(1)}, f32[2,2,64,3,128]{4,2,1,3,0:T(8,128)S(1)}, u32[]{:S(2)}, u32[]{:S(2)}) collective-permute-start(f32[2,2,64,3,128]{4,2,1,3,0:T(8,128)S(1)} %get-tuple-element.25), channel_id=1, source_target_pairs={{0,1},{1,2},{2,3},{3,4},{4,5},{5,6},{6,7},{7,8},{8,9},{9,10},{10,1... | collective-permute-start | bytes 1179656 | tf_op jit(solution)/shard_map/ppermute | solution.py:23
  77.3 26.2 %collective-permute-start.3 = (f32[2,2,64,3,128]{4,2,1,3,0:T(8,128)S(1)}, f32[2,2,64,3,128]{4,2,1,3,0:T(8,128)S(1)}, u32[]{:S(2)}, u32[]{:S(2)}) collective-permute-start(f32[2,2,64,3,128]{4,2,1,3,0:T(8,128)S(1)} %get-tuple-element.20), channel_id=1, source_target_pairs={{1,0},{2,1},{3,2},{4,3},{5,4},{6,5},{7,6},{8,7},{9,8},{10,9},{11,1... | collective-permute-start | bytes 1179656 | tf_op jit(solution)/shard_map/ppermute | solution.py:25
  86.2 25.4 %collective-permute-start.2 = (f32[2,2,64,3,128]{4,2,1,3,0:T(8,128)S(1)}, f32[2,2,64,3,128]{4,2,1,3,0:T(8,128)S(1)}, u32[]{:S(2)}, u32[]{:S(2)}) collective-permute-start(f32[2,2,64,3,128]{4,2,1,3,0:T(8,128)S(1)} %get-tuple-element.21), channel_id=1, source_target_pairs={{0,1},{1,2},{2,3},{3,4},{4,5},{5,6},{6,7},{7,8},{8,9},{9,10},{10,1... | collective-permute-start | bytes 1179656 | tf_op jit(solution)/shard_map/ppermute | solution.py:23
  115.9 15.0 %collective-permute-start.5 = (f32[2,2,64,3,128]{4,2,1,3,0:T(8,128)S(1)}, f32[2,2,64,3,128]{4,2,1,3,0:T(8,128)S(1)}, u32[]{:S(2)}, u32[]{:S(2)}) collective-permute-start(f32[2,2,64,3,128]{4,2,1,3,0:T(8,128)S(1)} %get-tuple-element.16), channel_id=1, source_target_pairs={{1,0},{2,1},{3,2},{4,3},{5,4},{6,5},{7,6},{8,7},{9,8},{10,9},{11,1... | collective-permute-start | bytes 1179656 | tf_op jit(solution)/shard_map/ppermute | solution.py:25
  123.3 30.2 %collective-permute-start.4 = (f32[2,2,64,3,128]{4,2,1,3,0:T(8,128)S(1)}, f32[2,2,64,3,128]{4,2,1,3,0:T(8,128)S(1)}, u32[]{:S(2)}, u32[]{:S(2)}) collective-permute-start(f32[2,2,64,3,128]{4,2,1,3,0:T(8,128)S(1)} %get-tuple-element.17), channel_id=1, source_target_pairs={{0,1},{1,2},{2,3},{3,4},{4,5},{5,6},{6,7},{7,8},{8,9},{9,10},{10,1... | collective-permute-start | bytes 1179656 | tf_op jit(solution)/shard_map/ppermute | solution.py:23
  168.1 508.4 %all-reduce.5.cloned.1.call-start = ((), (), s32[]{:S(2)}) async-start(), calls=%async_computation.3 | async-start | bytes 1048576 | tf_op jit(solution)/shard_map/psum | solution.py:133
  597.7 122.0 %reduce-scatter.2.cloned.1.call-start = ((), (), s32[]{:S(2)}) async-start(), calls=%async_computation.1 | async-start | bytes 2359296 | tf_op jit(solution)/shard_map/reduce_scatter | solution.py:122
Sparse Core Ops, SparseCore 0:
  168.2 429.4 all-reduce.2
  600.5 75.9 all-reduce.4
  679.6 40.0 reduce-scatter.1
